TPU v7x, 32 devices: a whole 2x2x4 slice. The times are simulated.
32 devices in a mesh: parts: 2 (over y), pool: 4 (over z), tp: 4 (over x, core).
Axes of the slice: x: 2, y: 2, z: 4, core: 2. Of those that a mesh axis runs over, the one named last changes fastest.
Arguments:
- queries: bfloat16 [4096, 8192], P(('parts', 'pool'), 'tp'), parts along dimension 0, may hold values from -400 to 400
- suffix_kv: bfloat16 [2, 8, 4096, 128], P(None, 'tp', ('parts', 'pool')), parts along dimension 2, may hold values from -12 to 12
- pool_kv: bfloat16 [2, 8, 64, 128, 128], P(None, 'tp', ('parts', 'pool')), parts along dimension 2, may hold values from -6 to 6
- prefix_pages: int32 [8], P('parts'), parts along dimension 0, may hold values from 1 to 4, as said below
- owner_start: int32 [8], P('parts'), parts along dimension 0, may hold values from 0 to 3
- page_slot: int32 [8, 4, 2], P('parts'), parts along dimension 0, may hold values from 0 to 7, as said below
Outputs:
- attention: bfloat16 [4096, 8192], P(('parts', 'pool'), 'tp'), parts along dimension 0
- new_pool: bfloat16 [2, 8, 64, 128, 128], P(None, 'tp', ('parts', 'pool')), parts along dimension 2
There are 2 independent parts, one for each index of `parts`. A program takes and returns all parts, laid end to end along the dimension named above; each array names one. Nothing has to cross between parts.
Inputs may be any that keep to these rules, and one draw needn't show every extreme that they name: For each owner o, the entries page_slot[:, o, :] name each of its 8 slots exactly once. `prefix_pages`: among the 4 requests of one serving group, at least one has exactly 4 prefix pages.
All inputs are finite; a program needn't handle non-finite values.
Results may differ from a plain program's by a relative error of at most 0.0035.
Values may be sent and summed in bfloat16 or wider, within the bound.
No kernel may reach another device: no remote copies, remote signals or barrier semaphores. Data moves between devices by JAX's collectives and lax.ppermute only.
A program may use at most 128 MiB of HBM per device.

v0:
```python
import functools
import math

import jax
import jax.numpy as jnp
from jax import lax
from jax.experimental import pallas as pl
from jax.experimental.pallas import tpu as pltpu
from jax.sharding import PartitionSpec as P

HBM = pl.BlockSpec(memory_space=pl.ANY)
VMEM = pl.BlockSpec(memory_space=pltpu.VMEM)
SMEM = pl.BlockSpec(memory_space=pltpu.SMEM)
TILE = 256


def partner(index, step, groups):
    if groups & (groups - 1):
        return (index + step) % groups, (index + groups - step) % groups
    return index ^ step, index ^ step


def fetch_kernel(slots_ref, pool_ref, *rest):
    sends, sems = rest[:-1], rest[-1]
    groups = slots_ref.shape[2]
    levels = sends[0].shape[0]
    me = lax.axis_index("pool")
    copies = []
    for step in range(groups - 1, 0, -1):
        dest = partner(me, step, groups)[0]
        for level in range(levels):
            slot = slots_ref[dest, level, me]
            copies.append(
                pltpu.make_async_copy(
                    pool_ref.at[:, :, slot], sends[step - 1].at[level], sems.at[step, level]
                )
            )
    for copy in copies:
        copy.start()
    for copy in copies:
        copy.wait()


def back_kernel(length_ref, start_ref, suffix_ref, *rest):
    sends, sems = rest[:-1], rest[-1]
    groups = len(sends)
    pages = suffix_ref.shape[2]
    me = lax.axis_index("pool")
    first = lax.rem(start_ref[me] + length_ref[me], groups)

    def each(act):
        for step in range(groups):
            offset = lax.rem(partner(me, step, groups)[0] + groups - first, groups)

            @pl.when(offset < pages)
            def _():
                act(
                    pltpu.make_async_copy(
                        suffix_ref.at[:, :, jnp.minimum(offset, pages - 1)],
                        sends[step],
                        sems.at[step],
                    )
                )

    each(lambda copy: copy.start())
    each(lambda copy: copy.wait())


def place_kernel(pages, length_ref, start_ref, slots_ref, *rest):
    backs, new_ref, sems = rest[:-3], rest[-2], rest[-1]
    _, levels, groups = slots_ref.shape
    me = lax.axis_index("pool")

    def each(act):
        for step in range(groups):
            request = partner(me, step, groups)[1]
            length = length_ref[request]
            first = lax.rem(start_ref[request] + length, groups)
            offset = lax.rem(me + groups - first, groups)

            @pl.when(offset < pages)
            def _():
                level = jnp.minimum(lax.div(length + offset, groups), levels - 1)
                slot = slots_ref[request, level, me]
                act(
                    pltpu.make_async_copy(backs[step], new_ref.at[:, :, slot], sems.at[step])
                )

    each(lambda copy: copy.start())
    each(lambda copy: copy.wait())


def attend_kernel(
    scale, per_step, length_ref, start_ref, slots_ref, query_ref, suffix_ref, pool_ref, *rest
):
    *page_refs, out_ref, new_ref, keys, values, sem = rest
    groups = slots_ref.shape[2]
    levels = page_refs[0].shape[0]
    page_len, head_dim = pool_ref.shape[3:]
    suffix = query_ref.shape[0]
    head, step = pl.program_id(0), pl.program_id(1)
    me = lax.axis_index("pool")
    copy = pltpu.make_async_copy(pool_ref, new_ref.at[:, pl.ds(head, 1)], sem)

    @pl.when(step == 0)
    def _():
        copy.start()
        length, first = length_ref[me], start_ref[me]
        keys[pl.ds(0, suffix), :] = suffix_ref[0, 0]
        values[pl.ds(0, suffix), pl.ds(0, head_dim)] = suffix_ref[1, 0]
        values[pl.ds(0, suffix), pl.ds(head_dim, head_dim)] = jnp.ones(
            (suffix, head_dim), values.dtype
        )
        for turn in range(groups):
            owner = partner(me, turn, groups)[1]
            for level in range(levels):
                rows = pl.ds(suffix + (turn * levels + level) * page_len, page_len)
                seen = level * groups + lax.rem(owner + groups - first, groups) < length

                @pl.when(seen)
                def _():
                    if turn:
                        keys[rows, :] = page_refs[turn - 1][level, 0, 0]
                        values[rows, pl.ds(0, head_dim)] = page_refs[turn - 1][level, 1, 0]
                    else:
                        slot = slots_ref[me, level, me]
                        keys[rows, :] = pool_ref[0, 0, slot]
                        values[rows, pl.ds(0, head_dim)] = pool_ref[1, 0, slot]
                    values[rows, pl.ds(head_dim, head_dim)] = jnp.ones(
                        (page_len, head_dim), values.dtype
                    )

                @pl.when(jnp.logical_not(seen))
                def _():
                    keys[rows, :] = jnp.broadcast_to(
                        suffix_ref[0, 0, pl.ds(0, 1), :], (page_len, head_dim)
                    )
                    values[rows, :] = jnp.zeros((page_len, 2 * head_dim), values.dtype)

    tile = min(TILE, suffix)
    total = keys.shape[0]
    seen = lax.broadcasted_iota(jnp.int32, (tile, tile), 1) <= lax.broadcasted_iota(
        jnp.int32, (tile, tile), 0
    )
    contract = (((1,), (1,)), ((), ()))
    dot = functools.partial(lax.dot_general, preferred_element_type=jnp.float32)
    plain = (((1,), (0,)), ((), ()))
    for column in range(per_step):
        lanes = pl.ds(column * head_dim, head_dim)
        for row in range(0, suffix, tile):
            query = query_ref[pl.ds(row, tile), lanes]
            parts = [
                (
                    jnp.where(
                        seen, dot(query, keys[pl.ds(row, tile), :], contract), -jnp.inf
                    ),
                    values[pl.ds(row, tile), :],
                )
            ]
            if row:
                parts.append((dot(query, keys[pl.ds(0, row), :], contract), values[pl.ds(0, row), :]))
            parts.append(
                (
                    dot(query, keys[pl.ds(suffix, total - suffix), :], contract),
                    values[pl.ds(suffix, total - suffix), :],
                )
            )
            top = functools.reduce(
                jnp.maximum, [jnp.max(score, axis=1, keepdims=True) for score, _ in parts]
            )
            mixed = None
            for score, value in parts:
                weight = jnp.exp2((score - top) * scale).astype(jnp.bfloat16)
                part = dot(weight, value, plain)
                mixed = part if mixed is None else mixed + part
            out_ref[pl.ds(row, tile), lanes] = (
                mixed[:, :head_dim] / mixed[:, head_dim:]
            ).astype(out_ref.dtype)

    @pl.when(step == pl.num_programs(1) - 1)
    def _():
        copy.wait()


def body(queries, suffix_kv, pool_kv, prefix_pages, owner_start, page_slot):
    _, heads, slots, page_len, head_dim = pool_kv.shape
    _, groups, levels = page_slot.shape
    suffix = queries.shape[0]
    per_kv = queries.shape[1] // (heads * head_dim)
    pages = suffix // page_len
    fetched = -(-(levels * groups - pages) // groups)
    page = (2, heads, page_len, head_dim)
    slot_of = jnp.swapaxes(page_slot, 1, 2)
    dtype = pool_kv.dtype

    def exchange(sends):
        arrived = [None] * (groups - 1)
        for step in range(groups - 1, 0, -1):
            pairs = [(index, partner(index, step, groups)[0]) for index in range(groups)]
            arrived[step - 1] = lax.ppermute(sends[step - 1], "pool", pairs)
        return arrived

    sends = pl.pallas_call(
        fetch_kernel,
        out_shape=[pltpu.VMEM((fetched,) + page, dtype)] * (groups - 1),
        in_specs=[SMEM, HBM],
        out_specs=[VMEM] * (groups - 1),
        scratch_shapes=[pltpu.SemaphoreType.DMA((groups, fetched))],
        name="gather_pages",
    )(slot_of, pool_kv)
    received = exchange(sends)

    own_back, *back_sends = pl.pallas_call(
        back_kernel,
        out_shape=[pltpu.VMEM(page, dtype)] * groups,
        in_specs=[SMEM, SMEM, HBM],
        out_specs=[VMEM] * groups,
        scratch_shapes=[pltpu.SemaphoreType.DMA((groups,))],
        name="pick_suffix",
    )(prefix_pages, owner_start, suffix_kv.reshape(2, heads, pages, page_len, head_dim))
    returned = exchange(back_sends)

    per_step = math.gcd(per_kv, 4)
    steps = per_kv // per_step
    total = suffix + fetched * groups * page_len
    result, new_pool = pl.pallas_call(
        functools.partial(attend_kernel, math.log2(math.e) / math.sqrt(head_dim), per_step),
        grid=(heads, steps),
        out_shape=(
            jax.ShapeDtypeStruct(queries.shape, dtype),
            jax.ShapeDtypeStruct(pool_kv.shape, dtype),
        ),
        in_specs=[
            SMEM,
            SMEM,
            SMEM,
            pl.BlockSpec((suffix, per_step * head_dim), lambda h, s: (0, h * steps + s)),
            pl.BlockSpec((2, 1, suffix, head_dim), lambda h, s: (0, h, 0, 0)),
            pl.BlockSpec((2, 1, slots, page_len, head_dim), lambda h, s: (0, h, 0, 0, 0)),
        ]
        + [pl.BlockSpec((fetched, 2, 1, page_len, head_dim), lambda h, s: (0, 0, h, 0, 0))]
        * (groups - 1),
        out_specs=(
            pl.BlockSpec((suffix, per_step * head_dim), lambda h, s: (0, h * steps + s)),
            HBM,
        ),
        scratch_shapes=[
            pltpu.VMEM((total, head_dim), dtype),
            pltpu.VMEM((total, 2 * head_dim), dtype),
            pltpu.SemaphoreType.DMA(()),
        ],
        compiler_params=pltpu.CompilerParams(vmem_limit_bytes=48 * 1024 * 1024),
        cost_estimate=pl.CostEstimate(
            flops=4 * heads * per_kv * suffix * total * head_dim,
            bytes_accessed=4 * queries.size + 8 * pool_kv.size,
            transcendentals=heads * per_kv * suffix * total,
        ),
        name="attend",
    )(prefix_pages, owner_start, slot_of, queries, suffix_kv, pool_kv, *received)

    new_pool = pl.pallas_call(
        functools.partial(place_kernel, pages),
        out_shape=jax.ShapeDtypeStruct(pool_kv.shape, dtype),
        in_specs=[SMEM, SMEM, SMEM] + [VMEM] * groups + [HBM],
        out_specs=HBM,
        input_output_aliases={3 + groups: 0},
        scratch_shapes=[pltpu.SemaphoreType.DMA((groups,))],
        name="place_pages",
    )(prefix_pages, owner_start, slot_of, own_back, *returned, new_pool)
    return (result, new_pool)


def solution(mesh):
    in_specs = (
        P(("parts", "pool"), "tp"),
        P(None, "tp", ("parts", "pool"), None),
        P(None, "tp", ("parts", "pool"), None, None),
        P("parts"),
        P("parts"),
        P("parts", None, None),
    )
    out_specs = (P(("parts", "pool"), "tp"), P(None, "tp", ("parts", "pool"), None, None))
    return jax.shard_map(body, mesh=mesh, in_specs=in_specs, out_specs=out_specs, check_vma=False)
```

profile of v0, /device:TPU:12, one launch (start us, length us, event | category | flops | bytes accessed | tf_op | source)
XLA Modules:
  0.0 47.7 jit_solution(5161252890102106066)
XLA Ops:
  0.6 1.8 %gather_pages.1 = (bf16[1,2,2,128,128]{4,3,2,1,0:T(8,128)(2,1)S(1)}, bf16[1,2,2,128,128]{4,3,2,1,0:T(8,128)(2,1)S(1)}, bf16[1,2,2,128,128]{4,3,2,1,0:T(8,128)(2,1)S(1)}) custom-call(s32[4,2,4]{2,1,0:T(2,128)} %bitcast.3, bf16[2,2,8,128,128]{4,3,2,1,0:T(8,128)(2,1)} %pool_ref.3), custom_call_target="tpu_custom_call" | custom-call | tf_op jit(solution)/shard_map/gather_pages/pallas_call | solution.py:203
  2.4 0.5 %collective-permute-start = (bf16[1,2,2,128,128]{4,3,2,1,0:T(8,128)(2,1)S(1)}, bf16[1,2,2,128,128]{4,3,2,1,0:T(8,128)(2,1)S(1)}, u32[]{:S(2)}, u32[]{:S(2)}) collective-permute-start(bf16[1,2,2,128,128]{4,3,2,1,0:T(8,128)(2,1)S(1)} %get-tuple-element.11), channel_id=1, source_target_pairs={{0,4},{4,0},{8,12},{12,8},{1,5},{5,1},{9,13},{13,9},{2,6},{6,2},{1... | collective-permute-start | bytes 393224 | tf_op jit(solution)/shard_map/ppermute | solution.py:200
  3.0 2.6 %collective-permute-start.1 = (bf16[1,2,2,128,128]{4,3,2,1,0:T(8,128)(2,1)S(1)}, bf16[1,2,2,128,128]{4,3,2,1,0:T(8,128)(2,1)S(1)}, u32[]{:S(2)}, u32[]{:S(2)}) collective-permute-start(bf16[1,2,2,128,128]{4,3,2,1,0:T(8,128)(2,1)S(1)} %get-tuple-element.12), channel_id=1, source_target_pairs={{0,8},{4,12},{8,0},{12,4},{1,9},{5,13},{9,1},{13,5},{2,10},{6,14},... | collective-permute-start | bytes 393224 | tf_op jit(solution)/shard_map/ppermute | solution.py:200
  5.5 0.5 collective-permute-start.2
  6.0 1.8 %pick_suffix.1 = (bf16[2,2,128,128]{3,2,1,0:T(8,128)(2,1)S(1)}, bf16[2,2,128,128]{3,2,1,0:T(8,128)(2,1)S(1)}, bf16[2,2,128,128]{3,2,1,0:T(8,128)(2,1)S(1)}, bf16[2,2,128,128]{3,2,1,0:T(8,128)(2,1)S(1)}) custom-call(s32[4]{0:T(128)} %length_ref.5, s32[4]{0:T(128)} %start_ref.5, bf16[2,2,4,128,128]{4,3,2,1,0:T(8,128)(2,1)} %bitcast.2), custom_call_target="tpu_custom_call" | custom-call | tf_op jit(solution)/shard_map/pick_suffix/pallas_call | solution.py:213
  7.8 0.0 copy-start.2
  7.8 1.4 %collective-permute-start.3 = (bf16[2,2,128,128]{3,2,1,0:T(8,128)(2,1)S(1)}, bf16[2,2,128,128]{3,2,1,0:T(8,128)(2,1)S(1)}, u32[]{:S(2)}, u32[]{:S(2)}) collective-permute-start(bf16[2,2,128,128]{3,2,1,0:T(8,128)(2,1)S(1)} %get-tuple-element.16), channel_id=1, source_target_pairs={{0,4},{4,0},{8,12},{12,8},{1,5},{5,1},{9,13},{13,9},{2,6},{6,2},{1... | collective-permute-start | bytes 393224 | tf_op jit(solution)/shard_map/ppermute | solution.py:200
  9.3 2.2 %collective-permute-start.4 = (bf16[2,2,128,128]{3,2,1,0:T(8,128)(2,1)S(1)}, bf16[2,2,128,128]{3,2,1,0:T(8,128)(2,1)S(1)}, u32[]{:S(2)}, u32[]{:S(2)}) collective-permute-start(bf16[2,2,128,128]{3,2,1,0:T(8,128)(2,1)S(1)} %get-tuple-element.17), channel_id=1, source_target_pairs={{0,8},{4,12},{8,0},{12,4},{1,9},{5,13},{9,1},{13,5},{2,10},{6,14},... | collective-permute-start | bytes 393224 | tf_op jit(solution)/shard_map/ppermute | solution.py:200
  11.5 0.0 collective-permute-done.rest_0_
  11.5 0.5 %collective-permute-start.5 = (bf16[2,2,128,128]{3,2,1,0:T(8,128)(2,1)S(1)}, bf16[2,2,128,128]{3,2,1,0:T(8,128)(2,1)S(1)}, u32[]{:S(2)}, u32[]{:S(2)}) collective-permute-start(bf16[2,2,128,128]{3,2,1,0:T(8,128)(2,1)S(1)} %get-tuple-element.18), channel_id=1, source_target_pairs={{0,12},{4,8},{8,4},{12,0},{1,13},{5,9},{9,5},{13,1},{2,14},{6,10},... | collective-permute-start | bytes 393224 | tf_op jit(solution)/shard_map/ppermute | solution.py:200
  12.0 3.2 %collective-permute-done.1.rest_1_ = bf16[1,2,2,128,128]{4,3,2,1,0:T(8,128)(2,1)S(1)} collective-permute-done((bf16[1,2,2,128,128]{4,3,2,1,0:T(8,128)(2,1)S(1)}, bf16[1,2,2,128,128]{4,3,2,1,0:T(8,128)(2,1)S(1)}, u32[]{:S(2)}, u32[]{:S(2)}) %collective-permute-start.1) | collective-permute-done | bytes 131104 | tf_op jit(solution)/shard_map/ppermute | solution.py:200
  15.2 9.3 %collective-permute-done.2.rest_2_ = bf16[1,2,2,128,128]{4,3,2,1,0:T(8,128)(2,1)S(1)} collective-permute-done((bf16[1,2,2,128,128]{4,3,2,1,0:T(8,128)(2,1)S(1)}, bf16[1,2,2,128,128]{4,3,2,1,0:T(8,128)(2,1)S(1)}, u32[]{:S(2)}, u32[]{:S(2)}) %collective-permute-start.2) | collective-permute-done | bytes 131104 | tf_op jit(solution)/shard_map/ppermute | solution.py:200
  24.4 0.0 copy-start
  24.4 1.2 %copy-done = bf16[2,2,8,128,128]{4,3,2,1,0:T(8,128)(2,1)S(1)} copy-done((bf16[2,2,8,128,128]{4,3,2,1,0:T(8,128)(2,1)S(1)}, bf16[2,2,8,128,128]{4,3,2,1,0:T(8,128)(2,1)}, u32[]{:S(2)}) %copy-start) | copy-done | bytes 1048600
  25.7 0.0 copy-start.1
  25.7 1.0 %copy-done.1 = bf16[2,2,512,128]{3,2,1,0:T(8,128)(2,1)S(1)} copy-done((bf16[2,2,512,128]{3,2,1,0:T(8,128)(2,1)S(1)}, bf16[2,2,512,128]{3,2,1,0:T(8,128)(2,1)}, u32[]{:S(2)}) %copy-start.1) | copy-done | bytes 524312
  26.7 0.0 copy-start.3
  26.7 0.7 %copy-done.3 = s32[4,4,2]{1,2,0:T(2,128)S(1)} copy-done((s32[4,4,2]{1,2,0:T(2,128)S(1)}, s32[4,4,2]{1,2,0:T(2,128)}, u32[]{:S(2)}) %copy-start.3) | copy-done | bytes 152
  27.4 0.0 copy-start.4
  27.4 0.7 %copy-done.4 = s32[4]{0:T(128)S(1)} copy-done((s32[4]{0:T(128)S(1)}, s32[4]{0:T(128)}, u32[]{:S(2)}) %copy-start.4) | copy-done | bytes 40
  28.1 0.0 copy-start.5
  28.1 0.7 %copy-done.5 = s32[4]{0:T(128)S(1)} copy-done((s32[4]{0:T(128)S(1)}, s32[4]{0:T(128)}, u32[]{:S(2)}) %copy-start.5) | copy-done | bytes 40
  28.7 0.0 copy-start.6
  28.7 1.6 %copy-done.6 = bf16[512,2048]{1,0:T(8,128)(2,1)S(1)} copy-done((bf16[512,2048]{1,0:T(8,128)(2,1)S(1)}, bf16[512,2048]{1,0:T(8,128)(2,1)}, u32[]{:S(2)}) %copy-start.6) | copy-done | bytes 2097176
  30.3 14.7 %attend.1 = (bf16[512,2048]{1,0:T(8,128)(2,1)}, bf16[2,2,8,128,128]{4,3,2,1,0:T(8,128)(2,1)}) custom-call(s32[4]{0:T(128)S(1)} %copy-done.4, s32[4]{0:T(128)S(1)} %copy-done.5, s32[4,2,4]{2,1,0:T(2,128)S(1)} %bitcast.5, bf16[512,2048]{1,0:T(8,128)(2,1)S(1)} %copy-done.6, bf16[2,2,512,128]{3,2,1,0:T(8,128)(2,1)S(1)} %copy-done.1, ...), custom_call_target="tpu_custom_call" | custom-call | flops 4294967296 | bytes 8388608 | tf_op jit(solution)/shard_map/attend/pallas_call | solution.py:226
  45.0 0.0 copy-done.2
  45.0 0.0 collective-permute-done.3.rest_1_
  45.0 0.0 copy-start.7
  45.0 0.0 collective-permute-done.4.rest_2_
  45.1 0.0 copy-start.8
  45.1 0.0 collective-permute-done.5.rest_3_
  45.1 0.0 copy-start.9
  45.1 0.6 %copy-done.7 = bf16[2,2,128,128]{3,2,1,0:T(8,128)(2,1)} copy-done((bf16[2,2,128,128]{3,2,1,0:T(8,128)(2,1)}, bf16[2,2,128,128]{3,2,1,0:T(8,128)(2,1)S(1)}, u32[]{:S(2)}) %copy-start.7) | copy-done | bytes 131096
  45.7 0.0 copy-done.8
  45.7 0.0 copy-done.9
  45.8 2.0 %place_pages.1 = bf16[2,2,8,128,128]{4,3,2,1,0:T(8,128)(2,1)} custom-call(s32[4]{0:T(128)} %length_ref.5, s32[4]{0:T(128)} %start_ref.5, s32[4,2,4]{2,1,0:T(2,128)} %bitcast.4, bf16[2,2,128,128]{3,2,1,0:T(8,128)(2,1)} %copy-done.2, bf16[2,2,128,128]{3,2,1,0:T(8,128)(2,1)} %copy-done.7, ...), custom_call_target="tpu_custom_call", output_to_operand_aliasing={{}: (7, {})} | custom-call | tf_op jit(solution)/shard_map/place_pages/pallas_call | solution.py:261
Async XLA Ops:
  2.4 9.0 %collective-permute-start = (bf16[1,2,2,128,128]{4,3,2,1,0:T(8,128)(2,1)S(1)}, bf16[1,2,2,128,128]{4,3,2,1,0:T(8,128)(2,1)S(1)}, u32[]{:S(2)}, u32[]{:S(2)}) collective-permute-start(bf16[1,2,2,128,128]{4,3,2,1,0:T(8,128)(2,1)S(1)} %get-tuple-element.11), channel_id=1, source_target_pairs={{0,4},{4,0},{8,12},{12,8},{1,5},{5,1},{9,13},{13,9},{2,6},{6,2},{1... | collective-permute-start | bytes 393224 | tf_op jit(solution)/shard_map/ppermute | solution.py:200
  3.0 12.2 %collective-permute-start.1 = (bf16[1,2,2,128,128]{4,3,2,1,0:T(8,128)(2,1)S(1)}, bf16[1,2,2,128,128]{4,3,2,1,0:T(8,128)(2,1)S(1)}, u32[]{:S(2)}, u32[]{:S(2)}) collective-permute-start(bf16[1,2,2,128,128]{4,3,2,1,0:T(8,128)(2,1)S(1)} %get-tuple-element.12), channel_id=1, source_target_pairs={{0,8},{4,12},{8,0},{12,4},{1,9},{5,13},{9,1},{13,5},{2,10},{6,14},... | collective-permute-start | bytes 393224 | tf_op jit(solution)/shard_map/ppermute | solution.py:200
  5.5 18.9 %collective-permute-start.2 = (bf16[1,2,2,128,128]{4,3,2,1,0:T(8,128)(2,1)S(1)}, bf16[1,2,2,128,128]{4,3,2,1,0:T(8,128)(2,1)S(1)}, u32[]{:S(2)}, u32[]{:S(2)}) collective-permute-start(bf16[1,2,2,128,128]{4,3,2,1,0:T(8,128)(2,1)S(1)} %get-tuple-element.13), channel_id=1, source_target_pairs={{0,12},{4,8},{8,4},{12,0},{1,13},{5,9},{9,5},{13,1},{2,14},{6,10},... | collective-permute-start | bytes 393224 | tf_op jit(solution)/shard_map/ppermute | solution.py:200
  7.8 37.2 %copy-start.2 = (bf16[2,2,128,128]{3,2,1,0:T(8,128)(2,1)}, bf16[2,2,128,128]{3,2,1,0:T(8,128)(2,1)S(1)}, u32[]{:S(2)}) copy-start(bf16[2,2,128,128]{3,2,1,0:T(8,128)(2,1)S(1)} %get-tuple-element.15.rest_0_) | copy-start | bytes 393220
  7.8 37.2 %collective-permute-start.3 = (bf16[2,2,128,128]{3,2,1,0:T(8,128)(2,1)S(1)}, bf16[2,2,128,128]{3,2,1,0:T(8,128)(2,1)S(1)}, u32[]{:S(2)}, u32[]{:S(2)}) collective-permute-start(bf16[2,2,128,128]{3,2,1,0:T(8,128)(2,1)S(1)} %get-tuple-element.16), channel_id=1, source_target_pairs={{0,4},{4,0},{8,12},{12,8},{1,5},{5,1},{9,13},{13,9},{2,6},{6,2},{1... | collective-permute-start | bytes 393224 | tf_op jit(solution)/shard_map/ppermute | solution.py:200
  9.3 35.8 %collective-permute-start.4 = (bf16[2,2,128,128]{3,2,1,0:T(8,128)(2,1)S(1)}, bf16[2,2,128,128]{3,2,1,0:T(8,128)(2,1)S(1)}, u32[]{:S(2)}, u32[]{:S(2)}) collective-permute-start(bf16[2,2,128,128]{3,2,1,0:T(8,128)(2,1)S(1)} %get-tuple-element.17), channel_id=1, source_target_pairs={{0,8},{4,12},{8,0},{12,4},{1,9},{5,13},{9,1},{13,5},{2,10},{6,14},... | collective-permute-start | bytes 393224 | tf_op jit(solution)/shard_map/ppermute | solution.py:200
  11.5 33.6 %collective-permute-start.5 = (bf16[2,2,128,128]{3,2,1,0:T(8,128)(2,1)S(1)}, bf16[2,2,128,128]{3,2,1,0:T(8,128)(2,1)S(1)}, u32[]{:S(2)}, u32[]{:S(2)}) collective-permute-start(bf16[2,2,128,128]{3,2,1,0:T(8,128)(2,1)S(1)} %get-tuple-element.18), channel_id=1, source_target_pairs={{0,12},{4,8},{8,4},{12,0},{1,13},{5,9},{9,5},{13,1},{2,14},{6,10},... | collective-permute-start | bytes 393224 | tf_op jit(solution)/shard_map/ppermute | solution.py:200
  24.4 1.2 %copy-start = (bf16[2,2,8,128,128]{4,3,2,1,0:T(8,128)(2,1)S(1)}, bf16[2,2,8,128,128]{4,3,2,1,0:T(8,128)(2,1)}, u32[]{:S(2)}) copy-start(bf16[2,2,8,128,128]{4,3,2,1,0:T(8,128)(2,1)} %pool_ref.3) | copy-start | bytes 3145732
  25.7 1.0 %copy-start.1 = (bf16[2,2,512,128]{3,2,1,0:T(8,128)(2,1)S(1)}, bf16[2,2,512,128]{3,2,1,0:T(8,128)(2,1)}, u32[]{:S(2)}) copy-start(bf16[2,2,512,128]{3,2,1,0:T(8,128)(2,1)} %suffix_ref.1) | copy-start | bytes 1572868
  26.7 0.7 %copy-start.3 = (s32[4,4,2]{1,2,0:T(2,128)S(1)}, s32[4,4,2]{1,2,0:T(2,128)}, u32[]{:S(2)}) copy-start(s32[4,4,2]{1,2,0:T(2,128)} %param.11) | copy-start | bytes 388
  27.4 0.7 %copy-start.4 = (s32[4]{0:T(128)S(1)}, s32[4]{0:T(128)}, u32[]{:S(2)}) copy-start(s32[4]{0:T(128)} %length_ref.5) | copy-start | bytes 52
  28.1 0.7 %copy-start.5 = (s32[4]{0:T(128)S(1)}, s32[4]{0:T(128)}, u32[]{:S(2)}) copy-start(s32[4]{0:T(128)} %start_ref.5) | copy-start | bytes 52
  28.7 1.6 %copy-start.6 = (bf16[512,2048]{1,0:T(8,128)(2,1)S(1)}, bf16[512,2048]{1,0:T(8,128)(2,1)}, u32[]{:S(2)}) copy-start(bf16[512,2048]{1,0:T(8,128)(2,1)} %query_ref.1) | copy-start | bytes 6291460
  45.0 0.7 %copy-start.7 = (bf16[2,2,128,128]{3,2,1,0:T(8,128)(2,1)}, bf16[2,2,128,128]{3,2,1,0:T(8,128)(2,1)S(1)}, u32[]{:S(2)}) copy-start(bf16[2,2,128,128]{3,2,1,0:T(8,128)(2,1)S(1)} %collective-permute-done.3.rest_1_) | copy-start | bytes 393220
  45.1 0.7 %copy-start.8 = (bf16[2,2,128,128]{3,2,1,0:T(8,128)(2,1)}, bf16[2,2,128,128]{3,2,1,0:T(8,128)(2,1)S(1)}, u32[]{:S(2)}) copy-start(bf16[2,2,128,128]{3,2,1,0:T(8,128)(2,1)S(1)} %collective-permute-done.4.rest_2_) | copy-start | bytes 393220
  45.1 0.7 %copy-start.9 = (bf16[2,2,128,128]{3,2,1,0:T(8,128)(2,1)}, bf16[2,2,128,128]{3,2,1,0:T(8,128)(2,1)S(1)}, u32[]{:S(2)}) copy-start(bf16[2,2,128,128]{3,2,1,0:T(8,128)(2,1)S(1)} %collective-permute-done.5.rest_3_) | copy-start | bytes 393220
where the time goes:
time: 48.1 us; the launch traced here: 47.7 us
  Pallas kernels  20.3 us (42%)
  waiting for transfers between devices  12.5 us (26%)
  starting transfers between devices  7.67 us (16%)
  local copies, waits for them, and re-layouts  6.56 us (14%)
  between operations  0.73 us (2%)
    pallas_call x1, Pallas kernels, body(): pl.pallas_call(functools.partial(attend_kernel, math.log2(math.e) / math....  14.7 us
    ppermute x6, waiting for transfers between devices, exchange(): arrived[step - 1] = lax.ppermute(sends[step - 1], 'pool', pairs)  12.5 us
    ppermute x6, starting transfers between devices, exchange(): arrived[step - 1] = lax.ppermute(sends[step - 1], 'pool', pairs)  7.67 us
    unnamed x20, local copies, waits for them, and re-layouts  6.56 us
    pallas_call x1, Pallas kernels, body(): pl.pallas_call(functools.partial(place_kernel, pages), out_shape=jax.Shap...  1.95 us
    pallas_call x1, Pallas kernels, body(): pl.pallas_call(back_kernel, out_shape=[pltpu.VMEM(page, dtype)] * groups,...  1.82 us
    pallas_call x1, Pallas kernels, body(): pl.pallas_call(fetch_kernel, out_shape=[pltpu.VMEM((fetched,) + page, dty...  1.81 us
  transfers between devices with their start and end apart: 6, of which 2 were waited for; matrix products, arithmetic and copies ran while one was open for 0% of the time, Pallas kernels for 35%

commit v1 on v0

v1 whole, which is shorter than its diff:
```python
import functools
import math

import jax
import jax.numpy as jnp
from jax import lax
from jax.experimental import pallas as pl
from jax.experimental.pallas import tpu as pltpu
from jax.sharding import PartitionSpec as P

HBM = pl.BlockSpec(memory_space=pl.ANY)
VMEM = pl.BlockSpec(memory_space=pltpu.VMEM)
SMEM = pl.BlockSpec(memory_space=pltpu.SMEM)
TILE = 256


def partner(index, step, groups):
    if groups & (groups - 1):
        return (index + step) % groups, (index + groups - step) % groups
    return index ^ step, index ^ step


def fetch_kernel(slots_ref, pool_ref, *rest):
    sends, sems = rest[:-1], rest[-1]
    groups = slots_ref.shape[2]
    levels = sends[0].shape[0]
    me = lax.axis_index("pool")
    copies = []
    for step in range(groups - 1, -1, -1):
        dest = partner(me, step, groups)[0]
        for level in range(levels):
            slot = slots_ref[dest, level, me]
            copies.append(
                pltpu.make_async_copy(
                    pool_ref.at[:, :, slot], sends[step].at[level], sems.at[step, level]
                )
            )
    for copy in copies:
        copy.start()
    for copy in copies:
        copy.wait()


def place_kernel(pages, length_ref, start_ref, slots_ref, *rest):
    backs, new_ref, sems = rest[:-4], rest[-2], rest[-1]
    _, levels, groups = slots_ref.shape
    me = lax.axis_index("pool")

    def each(act):
        for step in range(groups):
            request = partner(me, step, groups)[1]
            length = length_ref[request]
            first = lax.rem(start_ref[request] + length, groups)
            offset = lax.rem(me + groups - first, groups)

            @pl.when(offset < pages)
            def _():
                level = jnp.minimum(lax.div(length + offset, groups), levels - 1)
                slot = slots_ref[request, level, me]
                act(
                    pltpu.make_async_copy(backs[step], new_ref.at[:, :, slot], sems.at[step])
                )

    each(lambda copy: copy.start())
    each(lambda copy: copy.wait())


dot = functools.partial(lax.dot_general, preferred_element_type=jnp.float32)
ACROSS = (((1,), (1,)), ((), ()))
ALONG = (((1,), (0,)), ((), ()))


def suffix_kernel(
    scale, per_step, length_ref, start_ref, query_ref, suffix_ref, pool_ref, _, *rest
):
    sum_ref, stat_ref, new_ref, *back_refs, values, sem = rest
    groups = len(back_refs)
    page_len, head_dim = pool_ref.shape[3:]
    suffix = query_ref.shape[0]
    pages = suffix // page_len
    head, step = pl.program_id(0), pl.program_id(1)
    copy = pltpu.make_async_copy(pool_ref, new_ref.at[:, pl.ds(head, 1)], sem)

    @pl.when(step == 0)
    def _():
        copy.start()
        values[:, pl.ds(0, head_dim)] = suffix_ref[1, 0]
        values[:, pl.ds(head_dim, head_dim)] = jnp.ones((suffix, head_dim), values.dtype)
        me = lax.axis_index("pool")
        first = lax.rem(start_ref[me] + length_ref[me], groups)
        for turn in range(groups):
            offset = lax.rem(partner(me, turn, groups)[0] + groups - first, groups)
            row = pl.multiple_of(jnp.minimum(offset, pages - 1) * page_len, page_len)
            for side in range(2):
                back_refs[turn][side, 0] = suffix_ref[side, 0, pl.ds(row, page_len), :]

    tile = min(TILE, suffix)
    seen = lax.broadcasted_iota(jnp.int32, (tile, tile), 1) <= lax.broadcasted_iota(
        jnp.int32, (tile, tile), 0
    )
    lane = lax.broadcasted_iota(jnp.int32, (tile, head_dim), 1)
    for row in range(0, suffix, tile):
        rows = pl.ds(row, tile)
        stat = jnp.zeros((tile, head_dim), jnp.float32)
        for column in range(per_step):
            lanes = pl.ds(column * head_dim, head_dim)
            query = query_ref[rows, lanes]
            score = jnp.where(seen, dot(query, suffix_ref[0, 0, rows, :], ACROSS), -jnp.inf)
            top = jnp.max(score, axis=1, keepdims=True)
            if row:
                early = dot(query, suffix_ref[0, 0, pl.ds(0, row), :], ACROSS)
                top = jnp.maximum(top, jnp.max(early, axis=1, keepdims=True))
            mixed = dot(
                jnp.exp2((score - top) * scale).astype(jnp.bfloat16), values[rows, :], ALONG
            )
            if row:
                mixed += dot(
                    jnp.exp2((early - top) * scale).astype(jnp.bfloat16),
                    values[pl.ds(0, row), :],
                    ALONG,
                )
            sum_ref[rows, lanes] = mixed[:, :head_dim]
            stat = jnp.where(lane == column, top, stat)
            stat = jnp.where(lane == per_step + column, mixed[:, head_dim:], stat)
        stat_ref[0, rows, :] = stat

    @pl.when(step == pl.num_programs(1) - 1)
    def _():
        copy.wait()


def prefix_kernel(
    scale, per_step, length_ref, start_ref, query_ref, suffix_ref, sum_ref, stat_ref, *rest
):
    *page_refs, out_ref, keys, values = rest
    groups = len(page_refs)
    levels, _, _, page_len, head_dim = page_refs[0].shape
    suffix = query_ref.shape[0]

    @pl.when(pl.program_id(1) == 0)
    def _():
        me = lax.axis_index("pool")
        length, first = length_ref[me], start_ref[me]
        for turn in range(groups):
            owner = partner(me, turn, groups)[1]
            for level in range(levels):
                rows = pl.ds((turn * levels + level) * page_len, page_len)
                seen = level * groups + lax.rem(owner + groups - first, groups) < length

                @pl.when(seen)
                def _():
                    keys[rows, :] = page_refs[turn][level, 0, 0]
                    values[rows, pl.ds(0, head_dim)] = page_refs[turn][level, 1, 0]
                    values[rows, pl.ds(head_dim, head_dim)] = jnp.ones(
                        (page_len, head_dim), values.dtype
                    )

                @pl.when(jnp.logical_not(seen))
                def _():
                    keys[rows, :] = jnp.broadcast_to(
                        suffix_ref[0, 0, pl.ds(0, 1), :], (page_len, head_dim)
                    )
                    values[rows, :] = jnp.zeros((page_len, 2 * head_dim), values.dtype)

    tile = min(TILE, suffix)
    for column in range(per_step):
        lanes = pl.ds(column * head_dim, head_dim)
        for row in range(0, suffix, tile):
            rows = pl.ds(row, tile)
            score = dot(query_ref[rows, lanes], keys[...], ACROSS)
            before = stat_ref[0, rows, pl.ds(column, 1)]
            count = stat_ref[0, rows, pl.ds(per_step + column, 1)]
            top = jnp.maximum(before, jnp.max(score, axis=1, keepdims=True))
            factor = jnp.exp2((before - top) * scale)
            weight = jnp.exp2((score - top) * scale).astype(jnp.bfloat16)
            mixed = dot(weight, values[...], ALONG)
            total = mixed[:, head_dim:] + count * factor
            out_ref[rows, lanes] = (
                (mixed[:, :head_dim] + sum_ref[rows, lanes] * factor) / total
            ).astype(out_ref.dtype)


def body(queries, suffix_kv, pool_kv, prefix_pages, owner_start, page_slot):
    _, heads, slots, page_len, head_dim = pool_kv.shape
    _, groups, levels = page_slot.shape
    suffix = queries.shape[0]
    per_kv = queries.shape[1] // (heads * head_dim)
    pages = suffix // page_len
    fetched = -(-(levels * groups - pages) // groups)
    page = (2, heads, page_len, head_dim)
    slot_of = jnp.swapaxes(page_slot, 1, 2)
    dtype = pool_kv.dtype

    def exchange(sends):
        arrived = [sends[0]] + [None] * (groups - 1)
        for step in range(groups - 1, 0, -1):
            pairs = [(index, partner(index, step, groups)[0]) for index in range(groups)]
            arrived[step] = lax.ppermute(sends[step], "pool", pairs)
        return arrived

    sends = pl.pallas_call(
        fetch_kernel,
        out_shape=[pltpu.VMEM((fetched,) + page, dtype)] * groups,
        in_specs=[SMEM, HBM],
        out_specs=[VMEM] * groups,
        scratch_shapes=[pltpu.SemaphoreType.DMA((groups, fetched))],
        name="gather_pages",
    )(slot_of, pool_kv)
    received = exchange(sends)

    per_step = math.gcd(per_kv, 4)
    steps = per_kv // per_step
    scale = math.log2(math.e) / math.sqrt(head_dim)
    total = fetched * groups * page_len
    params = pltpu.CompilerParams(vmem_limit_bytes=60 * 1024 * 1024)
    columns = pl.BlockSpec((suffix, per_step * head_dim), lambda h, s: (0, h * steps + s))
    stats = pl.BlockSpec((1, suffix, head_dim), lambda h, s: (h * steps + s, 0, 0))

    def cost(keys):
        cells = heads * per_kv * suffix * keys
        return pl.CostEstimate(
            flops=6 * cells * head_dim, bytes_accessed=8 * queries.size, transcendentals=cells
        )

    sums, counts, new_pool, *back_sends = pl.pallas_call(
        functools.partial(suffix_kernel, scale, per_step),
        grid=(heads, steps),
        out_shape=[
            jax.ShapeDtypeStruct(queries.shape, jnp.float32),
            jax.ShapeDtypeStruct((heads * steps, suffix, head_dim), jnp.float32),
            jax.ShapeDtypeStruct(pool_kv.shape, dtype),
        ]
        + [jax.ShapeDtypeStruct(page, dtype)] * groups,
        in_specs=[
            SMEM,
            SMEM,
            columns,
            pl.BlockSpec((2, 1, suffix, head_dim), lambda h, s: (0, h, 0, 0)),
            pl.BlockSpec((2, 1, slots, page_len, head_dim), lambda h, s: (0, h, 0, 0, 0)),
            HBM,
        ],
        out_specs=[columns, stats, HBM]
        + [pl.BlockSpec((2, 1, page_len, head_dim), lambda h, s: (0, h, 0, 0))] * groups,
        scratch_shapes=[
            pltpu.VMEM((suffix, 2 * head_dim), dtype),
            pltpu.SemaphoreType.DMA(()),
        ],
        compiler_params=params,
        cost_estimate=cost(suffix),
        name="attend_suffix",
    )(prefix_pages, owner_start, queries, suffix_kv, pool_kv, sends[0])
    returned = exchange(back_sends)

    result = pl.pallas_call(
        functools.partial(prefix_kernel, scale, per_step),
        grid=(heads, steps),
        out_shape=jax.ShapeDtypeStruct(queries.shape, dtype),
        in_specs=[
            SMEM,
            SMEM,
            columns,
            pl.BlockSpec((1, 1, page_len, head_dim), lambda h, s: (0, h, 0, 0)),
            columns,
            stats,
        ]
        + [pl.BlockSpec((fetched, 2, 1, page_len, head_dim), lambda h, s: (0, 0, h, 0, 0))]
        * groups,
        out_specs=columns,
        scratch_shapes=[
            pltpu.VMEM((total, head_dim), dtype),
            pltpu.VMEM((total, 2 * head_dim), dtype),
        ],
        compiler_params=params,
        cost_estimate=cost(total),
        name="attend_prefix",
    )(prefix_pages, owner_start, queries, suffix_kv, sums, counts, *received)

    new_pool = pl.pallas_call(
        functools.partial(place_kernel, pages),
        out_shape=jax.ShapeDtypeStruct(pool_kv.shape, dtype),
        in_specs=[SMEM, SMEM, SMEM] + [VMEM] * groups + [HBM, HBM],
        out_specs=HBM,
        input_output_aliases={4 + groups: 0},
        scratch_shapes=[pltpu.SemaphoreType.DMA((groups,))],
        compiler_params=params,
        name="place_pages",
    )(prefix_pages, owner_start, slot_of, *returned, result, new_pool)
    return (result, new_pool)


def solution(mesh):
    in_specs = (
        P(("parts", "pool"), "tp"),
        P(None, "tp", ("parts", "pool"), None),
        P(None, "tp", ("parts", "pool"), None, None),
        P("parts"),
        P("parts"),
        P("parts", None, None),
    )
    out_specs = (P(("parts", "pool"), "tp"), P(None, "tp", ("parts", "pool"), None, None))
    return jax.shard_map(body, mesh=mesh, in_specs=in_specs, out_specs=out_specs, check_vma=False)
```

time: 48.1 us -> 43.3 us (0.900)
  the two profiles are of different devices: /device:TPU:12 before, /device:TPU:0 now
where the time goes in v1:
time: 43.3 us; the launch traced here: 43 us
  Pallas kernels  30.2 us (70%)
  starting transfers between devices  10.1 us (23%)
  local copies, waits for them, and re-layouts  2.06 us (5%)
  between operations  0.72 us (2%)
    pallas_call x1, Pallas kernels, body(): pl.pallas_call(functools.partial(prefix_kernel, scale, per_step), grid=(h...  17.6 us
    ppermute x6, starting transfers between devices, exchange(): arrived[step] = lax.ppermute(sends[step], 'pool', pairs)  10.1 us
    pallas_call x1, Pallas kernels, body(): pl.pallas_call(functools.partial(suffix_kernel, scale, per_step), grid=(h...  8.74 us
    unnamed x14, local copies, waits for them, and re-layouts  2.06 us
    pallas_call x1, Pallas kernels, body(): pl.pallas_call(functools.partial(place_kernel, pages), out_shape=jax.Shap...  1.95 us
    pallas_call x1, Pallas kernels, body(): pl.pallas_call(fetch_kernel, out_shape=[pltpu.VMEM((fetched,) + page, dty...  1.87 us
  transfers between devices with their start and end apart: 6, of which 0 were waited for; matrix products, arithmetic and copies ran while one was open for 0% of the time, Pallas kernels for 61%

profile of v1, /device:TPU:0, one launch (start us, length us, event | category | flops | bytes accessed | tf_op | source)
XLA Modules:
  0.0 43.0 jit_solution(10916691129104151995)
XLA Ops:
  0.6 1.9 %gather_pages.1 = (bf16[1,2,2,128,128]{4,3,2,1,0:T(8,128)(2,1)S(1)}, bf16[1,2,2,128,128]{4,3,2,1,0:T(8,128)(2,1)S(1)}, bf16[1,2,2,128,128]{4,3,2,1,0:T(8,128)(2,1)S(1)}, bf16[1,2,2,128,128]{4,3,2,1,0:T(8,128)(2,1)S(1)}) custom-call(s32[4,2,4]{2,1,0:T(2,128)} %bitcast.1, bf16[2,2,8,128,128]{4,3,2,1,0:T(8,128)(2,1)} %pool_ref.3), custom_call_target="tpu_custom_call" | custom-call | tf_op jit(solution)/shard_map/gather_pages/pallas_call | solution.py:201
  2.5 0.0 copy-start
  2.5 0.6 %copy-done = bf16[1,2,2,128,128]{4,3,2,1,0:T(8,128)(2,1)} copy-done((bf16[1,2,2,128,128]{4,3,2,1,0:T(8,128)(2,1)}, bf16[1,2,2,128,128]{4,3,2,1,0:T(8,128)(2,1)S(1)}, u32[]{:S(2)}) %copy-start) | copy-done | bytes 131096
  3.2 3.0 %collective-permute-start = (bf16[1,2,2,128,128]{4,3,2,1,0:T(8,128)(2,1)S(1)}, bf16[1,2,2,128,128]{4,3,2,1,0:T(8,128)(2,1)S(1)}, u32[]{:S(2)}, u32[]{:S(2)}) collective-permute-start(bf16[1,2,2,128,128]{4,3,2,1,0:T(8,128)(2,1)S(1)} %get-tuple-element.16), channel_id=1, source_target_pairs={{0,4},{4,0},{8,12},{12,8},{1,5},{5,1},{9,13},{13,9},{2,6},{6,2},{1... | collective-permute-start | bytes 393224 | tf_op jit(solution)/shard_map/ppermute | solution.py:198
  6.2 2.6 %collective-permute-start.1 = (bf16[1,2,2,128,128]{4,3,2,1,0:T(8,128)(2,1)S(1)}, bf16[1,2,2,128,128]{4,3,2,1,0:T(8,128)(2,1)S(1)}, u32[]{:S(2)}, u32[]{:S(2)}) collective-permute-start(bf16[1,2,2,128,128]{4,3,2,1,0:T(8,128)(2,1)S(1)} %get-tuple-element.17), channel_id=1, source_target_pairs={{0,8},{4,12},{8,0},{12,4},{1,9},{5,13},{9,1},{13,5},{2,10},{6,14},... | collective-permute-start | bytes 393224 | tf_op jit(solution)/shard_map/ppermute | solution.py:198
  8.8 0.0 collective-permute-start.2
  8.8 8.7 %attend_suffix.1 = (f32[512,2048]{1,0:T(8,128)}, f32[4,512,128]{2,1,0:T(8,128)}, bf16[2,2,8,128,128]{4,3,2,1,0:T(8,128)(2,1)}, bf16[2,2,128,128]{3,2,1,0:T(8,128...) custom-call(s32[4]{0:T(128)} %length_ref.5, ...), custom_call_target="tpu_custom_call" | custom-call | flops 3221225472 | bytes 8388608 | tf_op jit(solution)/shard_map/attend_suffix/pallas_call | solution.py:225
  17.5 0.9 %collective-permute-start.3 = (bf16[2,2,128,128]{3,2,1,0:T(8,128)(2,1)}, bf16[2,2,128,128]{3,2,1,0:T(8,128)(2,1)S(1)}, u32[]{:S(2)}, u32[]{:S(2)}) collective-permute-start(bf16[2,2,128,128]{3,2,1,0:T(8,128)(2,1)} %get-tuple-element.20), channel_id=1, source_target_pairs={{0,4},{4,0},{8,12},{12,8},{1,5},{5,1},{9,13},{13,9},{2,6},{6,2},{1... | collective-permute-start | bytes 393224 | tf_op jit(solution)/shard_map/ppermute | solution.py:198
  18.5 3.5 %collective-permute-start.4 = (bf16[2,2,128,128]{3,2,1,0:T(8,128)(2,1)}, bf16[2,2,128,128]{3,2,1,0:T(8,128)(2,1)S(1)}, u32[]{:S(2)}, u32[]{:S(2)}) collective-permute-start(bf16[2,2,128,128]{3,2,1,0:T(8,128)(2,1)} %get-tuple-element.21), channel_id=1, source_target_pairs={{0,8},{4,12},{8,0},{12,4},{1,9},{5,13},{9,1},{13,5},{2,10},{6,14},... | collective-permute-start | bytes 393224 | tf_op jit(solution)/shard_map/ppermute | solution.py:198
  22.0 0.0 collective-permute-done.rest_1_
  22.0 0.0 copy-start.4
  22.0 0.0 collective-permute-start.5
  22.0 0.0 collective-permute-done.1.rest_2_
  22.0 0.0 copy-start.5
  22.0 0.0 collective-permute-done.2.rest_3_
  22.0 0.0 copy-start.6
  22.0 0.6 %copy-done.4 = bf16[1,2,2,128,128]{4,3,2,1,0:T(8,128)(2,1)} copy-done((bf16[1,2,2,128,128]{4,3,2,1,0:T(8,128)(2,1)}, bf16[1,2,2,128,128]{4,3,2,1,0:T(8,128)(2,1)S(1)}, u32[]{:S(2)}) %copy-start.4) | copy-done | bytes 131096
  22.6 0.0 copy-done.5
  22.6 0.1 copy-done.6
  22.7 17.6 %attend_prefix.1.rest_4_ = bf16[512,2048]{1,0:T(8,128)(2,1)} custom-call(s32[4]{0:T(128)} %length_ref.5, s32[4]{0:T(128)} %start_ref.5, bf16[512,2048]{1,0:T(8,128)(2,1)} %query_ref.3, bf16[2,2,512,128]{3,2,1,0:T(8,128)(2,1)} %suffix_ref.3, f32[512,2048]{1,0:T(8,128)} %get-tuple-element.14.sum_ref, f32[4,512,128]{2,1,0:T(8,128)} %get-tuple-element.15.stat_ref, ...), custom_call_target="tpu_custom_call" | custom-call | flops 3221225472 | bytes 8388608 | tf_op jit(solution)/shard_map/attend_prefix/pallas_call | solution.py:254
  40.3 0.0 collective-permute-done.3.rest_1_
  40.3 0.0 copy-start.1
  40.4 0.0 collective-permute-done.4.rest_2_
  40.4 0.0 copy-start.2
  40.4 0.0 collective-permute-done.5.rest_3_
  40.4 0.0 copy-start.3
  40.4 0.6 %copy-done.1 = bf16[2,2,128,128]{3,2,1,0:T(8,128)(2,1)} copy-done((bf16[2,2,128,128]{3,2,1,0:T(8,128)(2,1)}, bf16[2,2,128,128]{3,2,1,0:T(8,128)(2,1)S(1)}, u32[]{:S(2)}) %copy-start.1) | copy-done | bytes 131096
  41.0 0.1 copy-done.2
  41.1 0.0 copy-done.3
  41.1 2.0 %place_pages.1 = bf16[2,2,8,128,128]{4,3,2,1,0:T(8,128)(2,1)} custom-call(s32[4]{0:T(128)} %length_ref.5, s32[4]{0:T(128)} %start_ref.5, s32[4,2,4]{2,1,0:T(2,128)} %bitcast.2, bf16[2,2,128,128]{3,2,1,0:T(8,128)(2,1)} %get-tuple-element.19.rest_0_, bf16[2,2,128,128]{3,2,1,0:T(8,128)(2,1)} %copy-done.1, ...), custom_call_target="tpu_custom_call", output_to_operand_aliasing={{}: (8, {})} | custom-call | tf_op jit(solution)/shard_map/place_pages/pallas_call | solution.py:278
Async XLA Ops:
  2.5 0.7 %copy-start = (bf16[1,2,2,128,128]{4,3,2,1,0:T(8,128)(2,1)}, bf16[1,2,2,128,128]{4,3,2,1,0:T(8,128)(2,1)S(1)}, u32[]{:S(2)}) copy-start(bf16[1,2,2,128,128]{4,3,2,1,0:T(8,128)(2,1)S(1)} %get-tuple-element.13._.rest_0_) | copy-start | bytes 393220
  3.2 18.8 %collective-permute-start = (bf16[1,2,2,128,128]{4,3,2,1,0:T(8,128)(2,1)S(1)}, bf16[1,2,2,128,128]{4,3,2,1,0:T(8,128)(2,1)S(1)}, u32[]{:S(2)}, u32[]{:S(2)}) collective-permute-start(bf16[1,2,2,128,128]{4,3,2,1,0:T(8,128)(2,1)S(1)} %get-tuple-element.16), channel_id=1, source_target_pairs={{0,4},{4,0},{8,12},{12,8},{1,5},{5,1},{9,13},{13,9},{2,6},{6,2},{1... | collective-permute-start | bytes 393224 | tf_op jit(solution)/shard_map/ppermute | solution.py:198
  6.2 15.8 %collective-permute-start.1 = (bf16[1,2,2,128,128]{4,3,2,1,0:T(8,128)(2,1)S(1)}, bf16[1,2,2,128,128]{4,3,2,1,0:T(8,128)(2,1)S(1)}, u32[]{:S(2)}, u32[]{:S(2)}) collective-permute-start(bf16[1,2,2,128,128]{4,3,2,1,0:T(8,128)(2,1)S(1)} %get-tuple-element.17), channel_id=1, source_target_pairs={{0,8},{4,12},{8,0},{12,4},{1,9},{5,13},{9,1},{13,5},{2,10},{6,14},... | collective-permute-start | bytes 393224 | tf_op jit(solution)/shard_map/ppermute | solution.py:198
  8.8 13.2 %collective-permute-start.2 = (bf16[1,2,2,128,128]{4,3,2,1,0:T(8,128)(2,1)S(1)}, bf16[1,2,2,128,128]{4,3,2,1,0:T(8,128)(2,1)S(1)}, u32[]{:S(2)}, u32[]{:S(2)}) collective-permute-start(bf16[1,2,2,128,128]{4,3,2,1,0:T(8,128)(2,1)S(1)} %get-tuple-element.18), channel_id=1, source_target_pairs={{0,12},{4,8},{8,4},{12,0},{1,13},{5,9},{9,5},{13,1},{2,14},{6,10},... | collective-permute-start | bytes 393224 | tf_op jit(solution)/shard_map/ppermute | solution.py:198
  17.5 22.8 %collective-permute-start.3 = (bf16[2,2,128,128]{3,2,1,0:T(8,128)(2,1)}, bf16[2,2,128,128]{3,2,1,0:T(8,128)(2,1)S(1)}, u32[]{:S(2)}, u32[]{:S(2)}) collective-permute-start(bf16[2,2,128,128]{3,2,1,0:T(8,128)(2,1)} %get-tuple-element.20), channel_id=1, source_target_pairs={{0,4},{4,0},{8,12},{12,8},{1,5},{5,1},{9,13},{13,9},{2,6},{6,2},{1... | collective-permute-start | bytes 393224 | tf_op jit(solution)/shard_map/ppermute | solution.py:198
  18.5 21.9 %collective-permute-start.4 = (bf16[2,2,128,128]{3,2,1,0:T(8,128)(2,1)}, bf16[2,2,128,128]{3,2,1,0:T(8,128)(2,1)S(1)}, u32[]{:S(2)}, u32[]{:S(2)}) collective-permute-start(bf16[2,2,128,128]{3,2,1,0:T(8,128)(2,1)} %get-tuple-element.21), channel_id=1, source_target_pairs={{0,8},{4,12},{8,0},{12,4},{1,9},{5,13},{9,1},{13,5},{2,10},{6,14},... | collective-permute-start | bytes 393224 | tf_op jit(solution)/shard_map/ppermute | solution.py:198
  22.0 0.7 %copy-start.4 = (bf16[1,2,2,128,128]{4,3,2,1,0:T(8,128)(2,1)}, bf16[1,2,2,128,128]{4,3,2,1,0:T(8,128)(2,1)S(1)}, u32[]{:S(2)}) copy-start(bf16[1,2,2,128,128]{4,3,2,1,0:T(8,128)(2,1)S(1)} %collective-permute-done.rest_1_) | copy-start | bytes 393220
  22.0 18.4 %collective-permute-start.5 = (bf16[2,2,128,128]{3,2,1,0:T(8,128)(2,1)}, bf16[2,2,128,128]{3,2,1,0:T(8,128)(2,1)S(1)}, u32[]{:S(2)}, u32[]{:S(2)}) collective-permute-start(bf16[2,2,128,128]{3,2,1,0:T(8,128)(2,1)} %get-tuple-element.22), channel_id=1, source_target_pairs={{0,12},{4,8},{8,4},{12,0},{1,13},{5,9},{9,5},{13,1},{2,14},{6,10},... | collective-permute-start | bytes 393224 | tf_op jit(solution)/shard_map/ppermute | solution.py:198
  22.0 0.7 %copy-start.5 = (bf16[1,2,2,128,128]{4,3,2,1,0:T(8,128)(2,1)}, bf16[1,2,2,128,128]{4,3,2,1,0:T(8,128)(2,1)S(1)}, u32[]{:S(2)}) copy-start(bf16[1,2,2,128,128]{4,3,2,1,0:T(8,128)(2,1)S(1)} %collective-permute-done.1.rest_2_) | copy-start | bytes 393220
  22.0 0.7 %copy-start.6 = (bf16[1,2,2,128,128]{4,3,2,1,0:T(8,128)(2,1)}, bf16[1,2,2,128,128]{4,3,2,1,0:T(8,128)(2,1)S(1)}, u32[]{:S(2)}) copy-start(bf16[1,2,2,128,128]{4,3,2,1,0:T(8,128)(2,1)S(1)} %collective-permute-done.2.rest_3_) | copy-start | bytes 393220
  40.3 0.7 %copy-start.1 = (bf16[2,2,128,128]{3,2,1,0:T(8,128)(2,1)}, bf16[2,2,128,128]{3,2,1,0:T(8,128)(2,1)S(1)}, u32[]{:S(2)}) copy-start(bf16[2,2,128,128]{3,2,1,0:T(8,128)(2,1)S(1)} %collective-permute-done.3.rest_1_) | copy-start | bytes 393220
  40.4 0.7 %copy-start.2 = (bf16[2,2,128,128]{3,2,1,0:T(8,128)(2,1)}, bf16[2,2,128,128]{3,2,1,0:T(8,128)(2,1)S(1)}, u32[]{:S(2)}) copy-start(bf16[2,2,128,128]{3,2,1,0:T(8,128)(2,1)S(1)} %collective-permute-done.4.rest_2_) | copy-start | bytes 393220
  40.4 0.7 %copy-start.3 = (bf16[2,2,128,128]{3,2,1,0:T(8,128)(2,1)}, bf16[2,2,128,128]{3,2,1,0:T(8,128)(2,1)S(1)}, u32[]{:S(2)}) copy-start(bf16[2,2,128,128]{3,2,1,0:T(8,128)(2,1)S(1)} %collective-permute-done.5.rest_3_) | copy-start | bytes 393220
